TPU v7x, 128 devices: a whole 4x4x4 slice. The times are simulated.
128 devices in a mesh: edge: 4 (over x), cols: 32 (over z, y, core).
Axes of the slice: x: 4, y: 4, z: 4, core: 2. Of those that a mesh axis runs over, the one named last changes fastest.
Arguments:
- atmos_state: bfloat16 [11, 128, 16, 4096], P(None, None, 'edge', 'cols'), may hold values from -5 to 6
- horiz_wind: float32 [2, 128, 16, 4096], P(None, None, 'edge', 'cols'), may hold values from -6 to 6
- route_map: int32 [16, 4096], P('edge', 'cols'), may hold values from 0 to 31, as said below
- diffusivity: float32 [128, 131072], P(None, ('edge', 'cols')), may hold values from 0.1 to 100
- branch_mask: int32 [128, 131072], P(None, ('edge', 'cols')), may hold values from 0 to 3
- phys_state: float32 [8, 128, 131072], P(None, None, ('edge', 'cols')), may hold values from -6 to 6
Outputs:
- new_state: bfloat16 [11, 128, 16, 4096], P(None, None, 'edge', 'cols')
- phys_next: float32 [8, 128, 131072], P(None, None, ('edge', 'cols'))
Inputs may be any that keep to these rules, and one draw needn't show every extreme that they name: `route_map`: on every device, at most 32 of its columns go to any one group, and exactly 32 go to one of them.
All inputs are finite; a program needn't handle non-finite values.
Results may differ from a plain program's by a relative error of at most 0.005.
Values may be sent and summed in bfloat16 or wider, within the bound.
A program may use at most 192 MiB of HBM per device.

v0:
```python
import functools

import jax
import jax.numpy as jnp
import numpy as np
from jax import lax
from jax.experimental import pallas as pl
from jax.experimental.pallas import tpu as pltpu
from jax.sharding import PartitionSpec as P

MESH = pl.DeviceIdType.MESH
F32, BF16 = jnp.float32, jnp.bfloat16
FIELDS, LEV, XD, YD = 11, 128, 4, 128
EDGE, COLS, CAP, PF = 4, 32, 32, 8
SLOTS = COLS * CAP
ROWS = LEV * XD
ALL_ROWS = FIELDS * ROWS
CHUNK = 128
CHUNKS = ALL_ROWS // CHUNK
CLEV = CHUNK // XD
YPAD = 48
PENALTY = 3.0
STEP_SIZE = 0.05
LATENT_WARM = 0.5
LATENT_ICE = 0.6
COUPLE_WARM = [0.8, -0.6, 0.5, 0.9, -0.7, 0.4, 1.0, -0.5]
COUPLE_ICE = [-0.4, 0.7, 0.9, -0.5, 0.6, -0.8, 0.3, 0.7]


def gll_matrix():
    nodes = np.array([-1.0, -1.0 / np.sqrt(5.0), 1.0 / np.sqrt(5.0), 1.0])
    prod = [np.prod([nodes[i] - nodes[j] for j in range(4) if j != i]) for i in range(4)]
    table = np.zeros((4, 4))
    for i in range(4):
        for j in range(4):
            if i != j:
                table[i, j] = prod[i] / (prod[j] * (nodes[i] - nodes[j]))
            else:
                table[i, i] = sum(1.0 / (nodes[i] - nodes[k]) for k in range(4) if k != i)
    return table


def split_bf16(table):
    high = table.astype(np.float32).astype(BF16)
    low = (table - high.astype(np.float64)).astype(np.float32).astype(BF16)
    return high, low


def constants():
    own = gll_matrix()
    own[0, 0] += PENALTY
    own[3, 3] -= PENALTY
    gx = np.zeros((CHUNK, CHUNK + 2 * CLEV))
    for lev in range(CLEV):
        gx[4 * lev : 4 * lev + 4, 4 * lev : 4 * lev + 4] = own
        gx[4 * lev, CHUNK + lev] = -PENALTY
        gx[4 * lev + 3, CHUNK + CLEV + lev] = PENALTY
    gy = np.zeros((YD, YD))
    for el in range(YD // 4):
        gy[4 * el : 4 * el + 4, 4 * el : 4 * el + 4] = own.T
        if el:
            gy[4 * el - 1, 4 * el] = -PENALTY
        if el < YD // 4 - 1:
            gy[4 * el + 4, 4 * el + 3] = PENALTY
    ey = np.zeros((YD, YD))
    ey[:YPAD, 0] = -PENALTY
    ey[YPAD : 2 * YPAD, YD - 1] = PENALTY
    pick = np.zeros((16, YD))
    pick[0, 0] = 1
    pick[8, YD - 1] = 1
    tri = np.triu(np.ones((YD, YD)), 1)
    eye = np.eye(128)
    gx = (-STEP_SIZE) * gx
    gy = (-STEP_SIZE) * gy
    ey = (-STEP_SIZE) * ey
    out = [*split_bf16(gx), *split_bf16(gy), *split_bf16(ey)]
    return out + [pick.astype(BF16), tri.astype(BF16), eye.astype(BF16)]


def far_first():
    def dist(k):
        z, y = k // 8, (k // 2) % 4
        return min(z, 4 - z) + min(y, 4 - y)

    return sorted(range(1, COLS), key=lambda k: -dist(k))


def softplus(x):
    return jnp.maximum(x, 0.0) + jnp.log1p(jnp.exp(-jnp.abs(x)))


def rates(phys0, phys1, mask):
    warm = jnp.where((mask & 1) == 1, softplus(phys0), 0.0)
    ice = jnp.where(mask >= 2, softplus(phys1), 0.0)
    return warm, ice


def dot(a, b):
    return jnp.dot(a, b, preferred_element_type=F32)


def dot_t(a, b):
    return lax.dot_general(a, b, (((1,), (1,)), ((), ())), preferred_element_type=F32)


def t_dot(a, b):
    return lax.dot_general(a, b, (((0,), (0,)), ((), ())), preferred_element_type=F32)


def exchange_kernel(
    q, route, kv, mask, phys, wind, gxh, gxl, gyh, gyl, eyh, eyl, pick, tri, eye,
    recv, tend, slots,
    snd, qf, xs, xr, ysf, ys, yr, ss, rs, hss, hrs,
):
    e, me = lax.axis_index("edge"), lax.axis_index("cols")
    core, yy, zz = me % 2, (me // 2) % 4, me // 8
    order = far_first()

    def peer(k):
        return ((zz + k // 8) % 4) * 8 + ((yy + (k // 2) % 4) % 4) * 2 + (core + k % 2) % 2

    up_x, down_x = (e + 1) % EDGE, (e + EDGE - 1) % EDGE
    up_y, down_y = (me + 1) % COLS, (me + COLS - 1) % COLS
    bar = pltpu.get_barrier_semaphore()
    for k in order:
        pl.semaphore_signal(bar, inc=1, device_id=(e, peer(k)), device_id_type=MESH)
    for to in (up_x, down_x):
        pl.semaphore_signal(bar, inc=1, device_id=(to, me), device_id_type=MESH)

    def tile(j, carry):
        lanes = pl.ds(pl.multiple_of(j * 128, 128), 128)
        warm, ice = rates(phys[0, :, lanes], phys[1, :, lanes], mask[:, lanes])
        for v, value in ((0, kv[:, lanes]), (2, warm), (3, ice)):
            turned = dot_t(eye[...], value.astype(BF16)).astype(BF16)
            snd[pl.ds(j * 4, 4), v] = turned.reshape(4, CAP, LEV)
        return carry

    lax.fori_loop(0, 8, tile, 0)

    dest_at = lax.broadcasted_iota(jnp.int32, (COLS, YD), 0)
    before = jnp.zeros((COLS, 1), F32)
    for x in range(XD):
        hot = dest_at == route[x : x + 1, :]
        hot_f = jnp.where(hot, 1.0, 0.0)
        earlier = dot(hot_f.astype(BF16), tri[...]) + before
        before = before + jnp.sum(hot_f, axis=1, keepdims=True)
        rank = jnp.sum(jnp.where(hot, earlier, 0.0), axis=0, keepdims=True)
        slots[x : x + 1, :] = route[x : x + 1, :] * CAP + rank.astype(jnp.int32)

    qf[...] = q[...].astype(F32)
    for i, x in enumerate((0, XD - 1)):
        xs[i] = qf[pl.ds(x, FIELDS * LEV, stride=XD), :].astype(BF16)
    slot_at = lax.broadcasted_iota(jnp.int32, (SLOTS, YD), 0)
    total = jnp.zeros((SLOTS, LEV), F32)
    for x in range(XD):
        hot = jnp.where(slot_at == slots[x : x + 1, :], 1.0, 0.0).astype(BF16)
        vapour = qf[pl.ds(ROWS + x, LEV, stride=XD), :].astype(BF16)
        total = total + dot_t(hot, vapour)
    snd[:, 1] = total.astype(BF16).reshape(COLS, CAP, LEV)

    def edge_points(c, carry):
        rows = pl.ds(pl.multiple_of(c * CHUNK, CHUNK), CHUNK)
        ends = dot_t(pick[...], q[rows, :])
        ysf[pl.ds(c, 1), :] = ends[0:1]
        ysf[pl.ds(YPAD + c, 1), :] = ends[8:9]
        return carry

    ysf[...] = jnp.zeros_like(ysf)
    lax.fori_loop(0, CHUNKS, edge_points, 0)
    ys[...] = ysf[...].astype(BF16)

    pl.semaphore_wait(bar, COLS - 1 + 2)
    copies = []
    for i, to in ((0, down_x), (1, up_x)):
        copies.append(
            pltpu.make_async_remote_copy(
                xs.at[i], xr.at[1 - i], hss.at[i], hrs.at[1 - i],
                device_id=(to, me), device_id_type=MESH,
            )
        )
    for i, to in ((0, down_y), (1, up_y)):
        copies.append(
            pltpu.make_async_remote_copy(
                ys.at[pl.ds(i * YPAD, YPAD)], yr.at[pl.ds((1 - i) * YPAD, YPAD)],
                hss.at[2 + i], hrs.at[3 - i],
                device_id=(e, to), device_id_type=MESH,
            )
        )
    for c in copies:
        c.start()

    def message(k):
        to = peer(k)
        return pltpu.make_async_remote_copy(
            snd.at[to], recv.at[me], ss.at[k], rs.at[k],
            device_id=(e, to), device_id_type=MESH,
        )

    for k in order:
        message(k).start()
    recv[pl.ds(me, 1)] = snd[pl.ds(me, 1)]
    yr[2 * YPAD :, :] = jnp.zeros((YD - 2 * YPAD, YD), BF16)
    for c in copies:
        c.wait()

    y_halo = dot_t(eye[...], yr[...])
    lane = lax.broadcasted_iota(jnp.int32, (CHUNK, YD), 1)

    def dynamics(c, carry):
        rows = pl.ds(pl.multiple_of(c * CHUNK, CHUNK), CHUNK)
        levels = pl.ds(pl.multiple_of(c * CLEV, CLEV), CLEV)
        wrows = pl.ds(pl.multiple_of((c % (ROWS // CHUNK)) * CHUNK, CHUNK), CHUNK)
        mine = q[rows, :]
        around = jnp.concatenate([mine, xr[0, levels], xr[1, levels]], axis=0)
        dx = dot(gxh[...], around) + dot(gxl[...], around)
        ends = jnp.where((lane == c) | (lane == YPAD + c), y_halo, 0.0).astype(BF16)
        dy = dot(mine, gyh[...]) + dot(mine, gyl[...])
        dy = dy + dot(ends, eyh[...]) + dot(ends, eyl[...])
        tend[rows, :] = (wind[0, wrows] * dx + wind[1, wrows] * dy).astype(BF16)
        return carry

    lax.fori_loop(0, CHUNKS, dynamics, 0)
    for k in order:
        message(k).wait()


def column_kernel(
    recv, slots, q, tend, kv, mask, phys, eye, new, phys_out, sol, cu, par, group, gkv, gcu
):
    slot_at = lax.broadcasted_iota(jnp.int32, (SLOTS, YD), 0)
    for x in range(XD):
        hot = jnp.where(slot_at == slots[x : x + 1, :], 1.0, 0.0).astype(BF16)
        for i, v in enumerate((0, 2, 3)):
            par[i, pl.ds(x * LEV, LEV), :] = t_dot(recv[:, v].reshape(SLOTS, LEV), hot)
    sol[...] = q[...].astype(F32)
    for j in range(8):
        rows = pl.ds(j * LEV, LEV)
        vapour = recv[pl.ds(j * 4, 4), 1].reshape(128, LEV)
        group[rows, :] = dot_t(eye[...], vapour)
        gkv[rows, :] = kv[:, j * 128 : (j + 1) * 128]

    def forward(k, carry):
        kv_t, cu_t, kv_g, cu_g, prev, prev_g = carry
        here = par[0, pl.ds(k, XD, stride=LEV), :]
        inv = 1.0 / (1.0 + here + kv_t - kv_t * cu_t)
        low = kv_t * inv
        cu_t = here * inv
        at = pl.multiple_of(k * XD, XD)
        cu[pl.ds(at, XD), :] = cu_t
        values = []
        for f in range(FIELDS):
            rows = pl.ds(f * ROWS + at, XD)
            value = sol[rows, :] * inv + low * prev[f]
            sol[rows, :] = value
            values.append(value)
        here_g = gkv[pl.ds(k, 8, stride=LEV), :]
        inv_g = 1.0 / (1.0 + here_g + kv_g - kv_g * cu_g)
        low_g = kv_g * inv_g
        cu_g = here_g * inv_g
        gcu[pl.ds(pl.multiple_of(k * 8, 8), 8), :] = cu_g
        value_g = group[pl.ds(k, 8, stride=LEV), :] * inv_g + low_g * prev_g
        group[pl.ds(k, 8, stride=LEV), :] = value_g
        return here, cu_t, here_g, cu_g, tuple(values), value_g

    zt, zg = jnp.zeros((XD, YD), F32), jnp.zeros((8, 128), F32)
    lax.fori_loop(0, LEV, forward, (zt, zt, zg, zg, (zt,) * FIELDS, zg), unroll=4)

    def backward(i, carry):
        after, after_g = carry
        k = LEV - 1 - i
        at = pl.multiple_of(k * XD, XD)
        cu_t = cu[pl.ds(at, XD), :]
        values = []
        for f in range(FIELDS):
            rows = pl.ds(f * ROWS + at, XD)
            value = sol[rows, :] + cu_t * after[f]
            sol[rows, :] = value
            values.append(value)
        cu_g = gcu[pl.ds(pl.multiple_of(k * 8, 8), 8), :]
        value_g = group[pl.ds(k, 8, stride=LEV), :] + cu_g * after_g
        group[pl.ds(k, 8, stride=LEV), :] = value_g
        return tuple(values), value_g

    lax.fori_loop(0, LEV, backward, ((zt,) * FIELDS, zg), unroll=4)

    for x in range(XD):
        warm, ice = par[1, pl.ds(x * LEV, LEV), :], par[2, pl.ds(x * LEV, LEV), :]
        inv = 1.0 / (1.0 + warm + ice)
        rows = [pl.ds(f * ROWS + x, LEV, stride=XD) for f in range(4)]
        passes = sol[rows[1], :] * (inv + inv * inv)
        to_warm, to_ice = warm * passes, ice * passes
        sol[rows[0], :] += LATENT_WARM * to_warm + LATENT_ICE * to_ice
        sol[rows[1], :] -= to_warm + to_ice
        sol[rows[2], :] += to_warm
        sol[rows[3], :] += to_ice
    new[...] = (sol[...] + tend[...].astype(F32)).astype(BF16)

    for j in range(8):
        lanes = slice(j * 128, (j + 1) * 128)
        warm, ice = rates(phys[0, :, lanes], phys[1, :, lanes], mask[:, lanes])
        inv = 1.0 / (1.0 + warm + ice)
        passes = group[j * LEV : (j + 1) * LEV, :] * (inv + inv * inv)
        warm, ice = warm * passes, ice * passes
        for f in range(PF):
            phys_out[f, :, lanes] = (
                phys[f, :, lanes] + COUPLE_WARM[f] * warm + COUPLE_ICE[f] * ice
            )


def shards(atmos_state, horiz_wind, route_map, diffusivity, branch_mask, phys_state):
    q = atmos_state.reshape(ALL_ROWS, YD)
    wind = horiz_wind.reshape(2, ROWS, YD)
    consts = [jnp.asarray(c) for c in constants()]
    whole = pl.BlockSpec(memory_space=pltpu.VMEM)
    recv, tend, slots = pl.pallas_call(
        exchange_kernel,
        grid=(1,),
        out_shape=(
            jax.ShapeDtypeStruct((COLS, 4, CAP, LEV), BF16),
            jax.ShapeDtypeStruct((ALL_ROWS, YD), BF16),
            jax.ShapeDtypeStruct((XD, YD), jnp.int32),
        ),
        in_specs=[whole] * 4
        + [pl.BlockSpec((2, LEV, SLOTS), lambda i: (0, 0, 0))]
        + [whole] * (1 + len(consts)),
        out_specs=(whole,) * 3,
        scratch_shapes=[
            pltpu.VMEM((COLS, 4, CAP, LEV), BF16),
            pltpu.VMEM((ALL_ROWS, YD), F32),
            pltpu.VMEM((2, FIELDS * LEV, YD), BF16),
            pltpu.VMEM((2, FIELDS * LEV, YD), BF16),
            pltpu.VMEM((2 * YPAD, YD), F32),
            pltpu.VMEM((2 * YPAD, YD), BF16),
            pltpu.VMEM((YD, YD), BF16),
            pltpu.SemaphoreType.DMA((COLS,)),
            pltpu.SemaphoreType.DMA((COLS,)),
            pltpu.SemaphoreType.DMA((4,)),
            pltpu.SemaphoreType.DMA((4,)),
        ],
        compiler_params=pltpu.CompilerParams(
            collective_id=0, has_side_effects=True, vmem_limit_bytes=40 << 20
        ),
    )(q, route_map, diffusivity, branch_mask, phys_state, wind, *consts)
    new, phys_next = pl.pallas_call(
        column_kernel,
        out_shape=(
            jax.ShapeDtypeStruct((ALL_ROWS, YD), BF16),
            jax.ShapeDtypeStruct((PF, LEV, SLOTS), F32),
        ),
        in_specs=[whole] * 8,
        out_specs=(whole,) * 2,
        scratch_shapes=[
            pltpu.VMEM((ALL_ROWS, YD), F32),
            pltpu.VMEM((ROWS, YD), F32),
            pltpu.VMEM((3, XD * LEV, YD), F32),
            pltpu.VMEM((8 * LEV, 128), F32),
            pltpu.VMEM((8 * LEV, 128), F32),
            pltpu.VMEM((8 * LEV, 128), F32),
        ],
        compiler_params=pltpu.CompilerParams(vmem_limit_bytes=40 << 20),
    )(recv, slots, q, tend, diffusivity, branch_mask, phys_state, consts[-1])
    return new.reshape(FIELDS, LEV, XD, YD), phys_next


def solution(mesh):
    return jax.shard_map(
        shards,
        mesh=mesh,
        in_specs=(
            P(None, None, "edge", "cols"),
            P(None, None, "edge", "cols"),
            P("edge", "cols"),
            P(None, ("edge", "cols")),
            P(None, ("edge", "cols")),
            P(None, None, ("edge", "cols")),
        ),
        out_specs=(P(None, None, "edge", "cols"), P(None, None, ("edge", "cols"))),
        check_vma=False,
    )
```

profile of v0, /device:TPU:1, one launch (start us, length us, event | category | flops | bytes accessed | tf_op | source)
XLA Modules:
  0.0 57.1 jit_solution(3535781662049597977)
XLA Ops:
  0.6 0.0 copy-start
  0.6 2.2 %copy-done = f32[8,128,1024]{2,1,0:T(8,128)S(1)} copy-done((f32[8,128,1024]{2,1,0:T(8,128)S(1)}, f32[8,128,1024]{2,1,0:T(8,128)}, u32[]{:S(2)}) %copy-start) | copy-done | bytes 4194328
  2.8 0.0 copy-start.2
  2.8 1.4 %copy-done.2 = bf16[11,128,4,128]{3,2,1,0:T(4,128)(2,1)S(1)} copy-done((bf16[11,128,4,128]{3,2,1,0:T(4,128)(2,1)S(1)}, bf16[11,128,4,128]{3,2,1,0:T(4,128)(2,1)}, u32[]{:S(2)}) %copy-start.2) | copy-done | bytes 1441816
  4.2 0.0 copy-start.3
  4.2 1.0 %copy-done.3 = f32[128,1024]{1,0:T(8,128)S(1)} copy-done((f32[128,1024]{1,0:T(8,128)S(1)}, f32[128,1024]{1,0:T(8,128)}, u32[]{:S(2)}) %copy-start.3) | copy-done | bytes 524312
  5.2 0.0 copy-start.5
  5.2 1.0 %copy-done.5 = s32[128,1024]{1,0:T(8,128)S(1)} copy-done((s32[128,1024]{1,0:T(8,128)S(1)}, s32[128,1024]{1,0:T(8,128)}, u32[]{:S(2)}) %copy-start.5) | copy-done | bytes 524312
  6.3 0.0 copy-start.6
  6.3 1.0 %copy-done.6 = f32[2,128,4,128]{3,2,1,0:T(4,128)S(1)} copy-done((f32[2,128,4,128]{3,2,1,0:T(4,128)S(1)}, f32[2,128,4,128]{3,2,1,0:T(4,128)}, u32[]{:S(2)}) %copy-start.6) | copy-done | bytes 524312
  7.3 0.0 copy-start.7
  7.3 0.8 %copy-done.7 = bf16[128,128]{1,0:T(8,128)(2,1)S(1)} copy-done((bf16[128,128]{1,0:T(8,128)(2,1)S(1)}, bf16[128,128]{1,0:T(8,128)(2,1)}, u32[]{:S(2)}) %copy-start.7) | copy-done | bytes 32792
  8.1 0.0 copy-start.8
  8.1 0.8 %copy-done.8 = bf16[128,192]{1,0:T(8,128)(2,1)S(1)} copy-done((bf16[128,192]{1,0:T(8,128)(2,1)S(1)}, bf16[128,192]{1,0:T(8,128)(2,1)}, u32[]{:S(2)}) %copy-start.8) | copy-done | bytes 49176
  8.9 0.0 copy-start.9
  8.9 0.8 %copy-done.9 = bf16[128,192]{1,0:T(8,128)(2,1)S(1)} copy-done((bf16[128,192]{1,0:T(8,128)(2,1)S(1)}, bf16[128,192]{1,0:T(8,128)(2,1)}, u32[]{:S(2)}) %copy-start.9) | copy-done | bytes 49176
  9.7 0.0 copy-start.10
  9.8 0.8 %copy-done.10 = bf16[128,128]{1,0:T(8,128)(2,1)S(1)} copy-done((bf16[128,128]{1,0:T(8,128)(2,1)S(1)}, bf16[128,128]{1,0:T(8,128)(2,1)}, u32[]{:S(2)}) %copy-start.10) | copy-done | bytes 32792
  10.5 0.0 copy-start.11
  10.5 0.8 %copy-done.11 = bf16[128,128]{1,0:T(8,128)(2,1)S(1)} copy-done((bf16[128,128]{1,0:T(8,128)(2,1)S(1)}, bf16[128,128]{1,0:T(8,128)(2,1)}, u32[]{:S(2)}) %copy-start.11) | copy-done | bytes 32792
  11.3 0.0 copy-start.12
  11.3 0.8 %copy-done.12 = bf16[128,128]{1,0:T(8,128)(2,1)S(1)} copy-done((bf16[128,128]{1,0:T(8,128)(2,1)S(1)}, bf16[128,128]{1,0:T(8,128)(2,1)}, u32[]{:S(2)}) %copy-start.12) | copy-done | bytes 32792
  12.0 0.0 copy-start.13
  12.0 0.8 %copy-done.13 = bf16[128,128]{1,0:T(8,128)(2,1)S(1)} copy-done((bf16[128,128]{1,0:T(8,128)(2,1)S(1)}, bf16[128,128]{1,0:T(8,128)(2,1)}, u32[]{:S(2)}) %copy-start.13) | copy-done | bytes 32792
  12.8 0.0 copy-start.14
  12.8 0.8 %copy-done.14 = bf16[128,128]{1,0:T(8,128)(2,1)S(1)} copy-done((bf16[128,128]{1,0:T(8,128)(2,1)S(1)}, bf16[128,128]{1,0:T(8,128)(2,1)}, u32[]{:S(2)}) %copy-start.14) | copy-done | bytes 32792
  13.5 0.0 copy-start.15
  13.5 0.7 %copy-done.15 = bf16[16,128]{1,0:T(8,128)(2,1)S(1)} copy-done((bf16[16,128]{1,0:T(8,128)(2,1)S(1)}, bf16[16,128]{1,0:T(8,128)(2,1)}, u32[]{:S(2)}) %copy-start.15) | copy-done | bytes 4120
  14.2 0.0 copy-start.16
  14.2 0.7 %copy-done.16 = s32[4,128]{1,0:T(4,128)S(1)} copy-done((s32[4,128]{1,0:T(4,128)S(1)}, s32[4,128]{1,0:T(4,128)}, u32[]{:S(2)}) %copy-start.16) | copy-done | bytes 2072
  14.9 0.0 copy-start.1
  14.9 0.0 copy-start.4
  14.9 31.8 %shard_map.158 = (bf16[32,4,32,128]{3,2,1,0:T(8,128)(2,1)S(1)}, bf16[5632,128]{1,0:T(8,128)(2,1)S(1)}, s32[4,128]{1,0:T(4,128)S(1)}) custom-call(bf16[5632,128]{1,0:T(8,128)(2,1)S(1)} %bitcast.3, s32[4,128]{1,0:T(4,128)S(1)} %copy-done.16, f32[128,1024]{1,0:T(8,128)S(1)} %copy-done.3, s32[128,1024]{1,0:T(8,128)S(1)} %copy-done.5, ...), custom_call_target="tpu_custom_call" | custom-call | tf_op jit(solution)/shard_map/pallas_call | solution.py:315
  46.7 0.0 copy-done.1
  46.7 0.0 copy-done.4
  46.7 10.4 %shard_map.159 = (bf16[5632,128]{1,0:T(8,128)(2,1)}, f32[8,128,1024]{2,1,0:T(8,128)}) custom-call(bf16[32,4,32,128]{3,2,1,0:T(8,128)(2,1)S(1)} %get-tuple-element.7.recv, s32[4,128]{1,0:T(4,128)S(1)} %get-tuple-element.8.slots, bf16[5632,128]{1,0:T(8,128)(2,1)S(1)} %bitcast.4, bf16[5632,128]{1,0:T(8,128)(2,1)S(1)} %get-tuple-element.9.tend, ...), custom_call_target="tpu_custom_call" | custom-call | tf_op jit(solution)/shard_map/pallas_call | solution.py:344
Async XLA Ops:
  0.6 2.2 %copy-start = (f32[8,128,1024]{2,1,0:T(8,128)S(1)}, f32[8,128,1024]{2,1,0:T(8,128)}, u32[]{:S(2)}) copy-start(f32[8,128,1024]{2,1,0:T(8,128)} %phys.3) | copy-start | bytes 12582916
  2.8 1.4 %copy-start.2 = (bf16[11,128,4,128]{3,2,1,0:T(4,128)(2,1)S(1)}, bf16[11,128,4,128]{3,2,1,0:T(4,128)(2,1)}, u32[]{:S(2)}) copy-start(bf16[11,128,4,128]{3,2,1,0:T(4,128)(2,1)} %param.15) | copy-start | bytes 4325380
  4.2 1.0 %copy-start.3 = (f32[128,1024]{1,0:T(8,128)S(1)}, f32[128,1024]{1,0:T(8,128)}, u32[]{:S(2)}) copy-start(f32[128,1024]{1,0:T(8,128)} %kv.3) | copy-start | bytes 1572868
  5.2 1.0 %copy-start.5 = (s32[128,1024]{1,0:T(8,128)S(1)}, s32[128,1024]{1,0:T(8,128)}, u32[]{:S(2)}) copy-start(s32[128,1024]{1,0:T(8,128)} %mask.3) | copy-start | bytes 1572868
  6.3 1.0 %copy-start.6 = (f32[2,128,4,128]{3,2,1,0:T(4,128)S(1)}, f32[2,128,4,128]{3,2,1,0:T(4,128)}, u32[]{:S(2)}) copy-start(f32[2,128,4,128]{3,2,1,0:T(4,128)} %param.16) | copy-start | bytes 1572868
  7.3 0.8 %copy-start.7 = (bf16[128,128]{1,0:T(8,128)(2,1)S(1)}, bf16[128,128]{1,0:T(8,128)(2,1)}, u32[]{:S(2)}) copy-start(bf16[128,128]{1,0:T(8,128)(2,1)} %constant.26.clone.eye) | copy-start | bytes 98308
  8.1 0.8 %copy-start.8 = (bf16[128,192]{1,0:T(8,128)(2,1)S(1)}, bf16[128,192]{1,0:T(8,128)(2,1)}, u32[]{:S(2)}) copy-start(bf16[128,192]{1,0:T(8,128)(2,1)} %constant.19.clone.gxl) | copy-start | bytes 147460
  8.9 0.8 %copy-start.9 = (bf16[128,192]{1,0:T(8,128)(2,1)S(1)}, bf16[128,192]{1,0:T(8,128)(2,1)}, u32[]{:S(2)}) copy-start(bf16[128,192]{1,0:T(8,128)(2,1)} %constant.18.clone.gxh) | copy-start | bytes 147460
  9.7 0.8 %copy-start.10 = (bf16[128,128]{1,0:T(8,128)(2,1)S(1)}, bf16[128,128]{1,0:T(8,128)(2,1)}, u32[]{:S(2)}) copy-start(bf16[128,128]{1,0:T(8,128)(2,1)} %constant.25.clone.tri) | copy-start | bytes 98308
  10.5 0.8 %copy-start.11 = (bf16[128,128]{1,0:T(8,128)(2,1)S(1)}, bf16[128,128]{1,0:T(8,128)(2,1)}, u32[]{:S(2)}) copy-start(bf16[128,128]{1,0:T(8,128)(2,1)} %constant.23.clone.eyl) | copy-start | bytes 98308
  11.3 0.8 %copy-start.12 = (bf16[128,128]{1,0:T(8,128)(2,1)S(1)}, bf16[128,128]{1,0:T(8,128)(2,1)}, u32[]{:S(2)}) copy-start(bf16[128,128]{1,0:T(8,128)(2,1)} %constant.22.clone.eyh) | copy-start | bytes 98308
  12.0 0.8 %copy-start.13 = (bf16[128,128]{1,0:T(8,128)(2,1)S(1)}, bf16[128,128]{1,0:T(8,128)(2,1)}, u32[]{:S(2)}) copy-start(bf16[128,128]{1,0:T(8,128)(2,1)} %constant.21.clone.gyl) | copy-start | bytes 98308
  12.8 0.8 %copy-start.14 = (bf16[128,128]{1,0:T(8,128)(2,1)S(1)}, bf16[128,128]{1,0:T(8,128)(2,1)}, u32[]{:S(2)}) copy-start(bf16[128,128]{1,0:T(8,128)(2,1)} %constant.20.clone.gyh) | copy-start | bytes 98308
  13.5 0.7 %copy-start.15 = (bf16[16,128]{1,0:T(8,128)(2,1)S(1)}, bf16[16,128]{1,0:T(8,128)(2,1)}, u32[]{:S(2)}) copy-start(bf16[16,128]{1,0:T(8,128)(2,1)} %constant.24.clone.pick) | copy-start | bytes 12292
  14.2 0.7 %copy-start.16 = (s32[4,128]{1,0:T(4,128)S(1)}, s32[4,128]{1,0:T(4,128)}, u32[]{:S(2)}) copy-start(s32[4,128]{1,0:T(4,128)} %route.1) | copy-start | bytes 6148
  14.9 31.8 %copy-start.1 = (f32[8,128,1024]{2,1,0:T(8,128)S(1)}, f32[8,128,1024]{2,1,0:T(8,128)}, u32[]{:S(2)}) copy-start(f32[8,128,1024]{2,1,0:T(8,128)} %phys.3) | copy-start | bytes 12582916
  14.9 31.8 %copy-start.4 = (f32[128,1024]{1,0:T(8,128)S(1)}, f32[128,1024]{1,0:T(8,128)}, u32[]{:S(2)}) copy-start(f32[128,1024]{1,0:T(8,128)} %kv.3) | copy-start | bytes 1572868
where the time goes:
time: 58 us; the launch traced here: 57.1 us
  Pallas kernels  42.2 us (73%)
  local copies, waits for them, and re-layouts  14.3 us (25%)
  between operations  0.68 us (1%)
    pallas_call x1, Pallas kernels, shards(): pl.pallas_call(exchange_kernel, grid=(1,), out_shape=(jax.ShapeDtypeStruc...  31.8 us
    unnamed x34, local copies, waits for them, and re-layouts  14.3 us
    pallas_call x1, Pallas kernels, shards(): pl.pallas_call(column_kernel, out_shape=(jax.ShapeDtypeStruct((ALL_ROWS,...  10.4 us

commit v1 on v0

v1 whole, which is shorter than its diff:
```python
import functools

import jax
import jax.numpy as jnp
import numpy as np
from jax import lax
from jax.experimental import pallas as pl
from jax.experimental.pallas import tpu as pltpu
from jax.sharding import PartitionSpec as P

MESH = pl.DeviceIdType.MESH
F32, BF16 = jnp.float32, jnp.bfloat16
FIELDS, LEV, XD, YD = 11, 128, 4, 128
EDGE, COLS, CAP, PF = 4, 32, 32, 8
SLOTS = COLS * CAP
ROWS = LEV * XD
ALL_ROWS = FIELDS * ROWS
TOP = 4
YPAD = 16
PENALTY = 3.0
STEP_SIZE = 0.05
LATENT_WARM = 0.5
LATENT_ICE = 0.6
COUPLE_WARM = [0.8, -0.6, 0.5, 0.9, -0.7, 0.4, 1.0, -0.5]
COUPLE_ICE = [-0.4, 0.7, 0.9, -0.5, 0.6, -0.8, 0.3, 0.7]


def gll_matrix():
    nodes = np.array([-1.0, -1.0 / np.sqrt(5.0), 1.0 / np.sqrt(5.0), 1.0])
    prod = [np.prod([nodes[i] - nodes[j] for j in range(4) if j != i]) for i in range(4)]
    table = np.zeros((4, 4))
    for i in range(4):
        for j in range(4):
            if i != j:
                table[i, j] = prod[i] / (prod[j] * (nodes[i] - nodes[j]))
            else:
                table[i, i] = sum(1.0 / (nodes[i] - nodes[k]) for k in range(4) if k != i)
    return table


def split_bf16(table):
    high = table.astype(np.float32).astype(BF16)
    low = (table - high.astype(np.float64)).astype(np.float32).astype(BF16)
    return high, low


def derivative():
    own = gll_matrix()
    own[0, 0] += PENALTY
    own[3, 3] -= PENALTY
    return -STEP_SIZE * own


def constants():
    own = derivative() / -STEP_SIZE
    gy = np.zeros((YD, YD))
    for el in range(YD // 4):
        gy[4 * el : 4 * el + 4, 4 * el : 4 * el + 4] = own.T
        if el:
            gy[4 * el - 1, 4 * el] = -PENALTY
        if el < YD // 4 - 1:
            gy[4 * el + 4, 4 * el + 3] = PENALTY
    ey = np.zeros((YD, YD))
    ey[:YPAD, 0] = -PENALTY
    ey[YPAD : 2 * YPAD, YD - 1] = PENALTY
    table = np.concatenate(split_bf16(-STEP_SIZE * np.concatenate([gy, ey], 0)), 1)
    tri = np.triu(np.ones((YD, YD)), 1)
    square = np.concatenate([tri, np.eye(128)], 1).astype(BF16)
    return np.concatenate([table, square], 0)


def far_first():
    def dist(k):
        z, y = k // 8, (k // 2) % 4
        return min(z, 4 - z) + min(y, 4 - y)

    return sorted(range(1, COLS), key=lambda k: -dist(k))


def softplus(x):
    return jnp.maximum(x, 0.0) + jnp.log1p(jnp.exp(-jnp.abs(x)))


def rates(phys0, phys1, mask):
    warm = jnp.where((mask & 1) == 1, softplus(phys0), 0.0)
    ice = jnp.where(mask >= 2, softplus(phys1), 0.0)
    return warm, ice


def dot(a, b):
    return jnp.dot(a, b, preferred_element_type=F32)


def dot_t(a, b):
    return lax.dot_general(a, b, (((1,), (1,)), ((), ())), preferred_element_type=F32)


def t_dot(a, b):
    return lax.dot_general(a, b, (((0,), (0,)), ((), ())), preferred_element_type=F32)


def exchange_kernel(
    q_h, route_h, kv_h, mask_h, phys_h, wind_h, const_h,
    recv_b, hot, pre, vap, rest, phys,
    qv, route, kv, mask, wind, const, group, in_sem,
    snd_a, snd_b, recv_a, sol, qp, tn, xr, ys, yr, wp, par, cu, gkv, gcu,
    ss, rs, hss, hrs,
):
    e, me = lax.axis_index("edge"), lax.axis_index("cols")
    core, yy, zz = me % 2, (me // 2) % 4, me // 8
    order = far_first()

    def peer(k):
        return ((zz + k // 8) % 4) * 8 + ((yy + (k // 2) % 4) % 4) * 2 + (core + k % 2) % 2

    up_x, down_x = (e + 1) % EDGE, (e + EDGE - 1) % EDGE
    up_y, down_y = (me + 1) % COLS, (me + COLS - 1) % COLS
    loads = [
        pltpu.make_async_copy(a, b, in_sem.at[i])
        for i, (a, b) in enumerate(
            (
                (const_h, const), (kv_h, kv), (route_h, route), (q_h, qv),
                (mask_h, mask), (phys_h, phys), (wind_h, wind),
            )
        )
    ]
    for c in loads:
        c.start()
    bar = pltpu.get_barrier_semaphore()
    for k in order:
        pl.semaphore_signal(bar, inc=1, device_id=(e, peer(k)), device_id_type=MESH)
    for to in (up_x, down_x):
        pl.semaphore_signal(bar, inc=1, device_id=(to, me), device_id_type=MESH)
    tri = const.at[pl.ds(256, 128), pl.ds(0, 128)]
    eye = const.at[pl.ds(256, 128), pl.ds(128, 128)]

    def turn(j, value):
        turned = dot_t(eye[...], value.astype(BF16)).astype(BF16)
        return turned.reshape(4, CAP, LEV)

    loads[0].wait()
    loads[1].wait()
    for j in range(8):
        snd_a[4 * j : 4 * j + 4, 0] = turn(j, kv[:, j * 128 : (j + 1) * 128])

    loads[2].wait()
    dest_at = lax.broadcasted_iota(jnp.int32, (COLS, YD), 0)
    slot_at = lax.broadcasted_iota(jnp.int32, (SLOTS, YD), 0)
    before = jnp.zeros((COLS, 1), F32)
    for x in range(XD):
        chosen = dest_at == route[x : x + 1, :]
        chosen_f = jnp.where(chosen, 1.0, 0.0)
        earlier = dot(chosen_f.astype(BF16), tri[...]) + before
        before = before + jnp.sum(chosen_f, axis=1, keepdims=True)
        rank = jnp.sum(jnp.where(chosen, earlier, 0.0), axis=0, keepdims=True)
        slots = route[x : x + 1, :] * CAP + rank.astype(jnp.int32)
        hot[:, x * YD : (x + 1) * YD] = jnp.where(slot_at == slots, 1.0, 0.0).astype(BF16)

    loads[3].wait()

    def planes(f, carry):
        rows = pl.ds(pl.multiple_of(f * ROWS, ROWS), ROWS)
        sol[rows, :] = qv[rows, :].astype(F32)
        for x in range(XD):
            qp[f, x] = sol[pl.ds(f * ROWS + x, LEV, stride=XD), :].astype(BF16)
        return carry

    lax.fori_loop(0, FIELDS, planes, 0)
    total = dot_t(hot[...], jnp.concatenate([qp[1, x] for x in range(XD)], axis=1))
    snd_a[:, 1] = total.astype(BF16).reshape(COLS, CAP, LEV)

    fields = jnp.concatenate([qp[f].reshape(ROWS, YD) for f in range(FIELDS)], axis=1)
    at = lax.broadcasted_iota(jnp.int32, (YD, YD), 0)
    lane = lax.broadcasted_iota(jnp.int32, (YD, YD), 1)
    pick = [
        jnp.where(((at == 0) & (lane == f)) | ((at == YD - 1) & (lane == YPAD + f)), 1.0, 0.0)
        for f in range(FIELDS)
    ]
    ends = dot(fields, jnp.concatenate(pick, axis=0).astype(BF16)).astype(BF16)
    ys[...] = dot_t(eye[0 : 2 * YPAD, :], ends).astype(BF16)

    pl.semaphore_wait(bar, COLS - 1 + 2)
    y_copies, x_copies = [], []
    for i, to in ((0, down_y), (1, up_y)):
        y_copies.append(
            pltpu.make_async_remote_copy(
                ys.at[pl.ds(i * YPAD, YPAD)], yr.at[pl.ds((1 - i) * YPAD, YPAD)],
                hss.at[2 + i], hrs.at[3 - i],
                device_id=(e, to), device_id_type=MESH,
            )
        )
    for i, to in ((0, down_x), (1, up_x)):
        x_copies.append(
            pltpu.make_async_remote_copy(
                qp.at[:, i * (XD - 1)], xr.at[1 - i], hss.at[i], hrs.at[1 - i],
                device_id=(to, me), device_id_type=MESH,
            )
        )
    for c in y_copies + x_copies:
        c.start()

    def message(k, part):
        to = peer(k)
        source, target = ((snd_a, recv_a), (snd_b, recv_b))[part]
        return pltpu.make_async_remote_copy(
            source.at[to], target.at[me], ss.at[part, k], rs.at[part, k],
            device_id=(e, to), device_id_type=MESH,
        )

    for k in order:
        message(k, 0).start()
    loads[4].wait()
    loads[5].wait()
    for j in range(8):
        lanes = slice(j * 128, (j + 1) * 128)
        warm, ice = rates(phys[0, :, lanes], phys[1, :, lanes], mask[:, lanes])
        snd_b[4 * j : 4 * j + 4, 0] = turn(j, warm)
        snd_b[4 * j : 4 * j + 4, 1] = turn(j, ice)
    for k in order:
        message(k, 1).start()
    recv_a[pl.ds(me, 1)] = snd_a[pl.ds(me, 1)]
    recv_b[pl.ds(me, 1)] = snd_b[pl.ds(me, 1)]

    loads[6].wait()
    for i in range(2):
        for x in range(XD):
            wp[i, x] = wind[i, pl.ds(x, LEV, stride=XD), :]
    for c in y_copies:
        c.wait()
    y_halo = t_dot(yr[...], eye[0 : 2 * YPAD, :])
    wide = lax.broadcasted_iota(jnp.int32, (ROWS, YD), 1)
    along = derivative()

    def dynamics(f, carry):
        near = jnp.where((wide == f) | (wide == YPAD + f), y_halo, 0.0).astype(BF16)
        both = jnp.concatenate([qp[f].reshape(ROWS, YD), near], axis=1)
        dy = dot(both, const[0:256, :])
        own = [qp[f, x].astype(F32) for x in range(XD)]
        for x in range(XD):
            dx = sum(float(along[x, i]) * own[i] for i in range(XD) if abs(along[x, i]) > 1e-9)
            rows = slice(x * LEV, (x + 1) * LEV)
            tn[pl.ds(f * ROWS + x, LEV, stride=XD), :] = wp[0, x] * dx + wp[1, x] * (
                dy[rows, :YD] + dy[rows, YD:]
            )
        return carry

    lax.fori_loop(0, FIELDS, dynamics, 0)

    for k in order:
        message(k, 0).wait()
    here = t_dot(recv_a[:, 0].reshape(SLOTS, LEV), hot[...])
    for x in range(XD):
        par[x * LEV : (x + 1) * LEV, :] = here[:, x * YD : (x + 1) * YD]
    for j in range(8):
        rows = pl.ds(j * LEV, LEV)
        group[rows, :] = dot_t(eye[...], recv_a[4 * j : 4 * j + 4, 1].reshape(128, LEV))
        gkv[rows, :] = kv[:, j * 128 : (j + 1) * 128]
    solve(sol, par, cu, group, gkv, gcu)

    for c in x_copies:
        c.wait()

    def corrections(f, carry):
        for i, x, sign in ((0, 0, 1.0), (1, XD - 1, -1.0)):
            rows = pl.ds(f * ROWS + x, LEV, stride=XD)
            tn[rows, :] += (sign * STEP_SIZE * PENALTY) * wp[0, x] * xr[i, f].astype(F32)
        return carry

    lax.fori_loop(0, FIELDS, corrections, 0)
    top = TOP * ROWS
    pre[...] = sol[:top, :] + tn[:top, :]
    for x in range(XD):
        vap[x] = sol[pl.ds(ROWS + x, LEV, stride=XD), :]
    rest[...] = (sol[top:, :] + tn[top:, :]).astype(BF16)
    couple(phys, mask, group)
    for k in order:
        message(k, 1).wait()


def solve(sol, par, cu, group, gkv, gcu):
    def forward(k, carry):
        kv_t, cu_t, kv_g, cu_g, prev, prev_g = carry
        here = par[pl.ds(k, XD, stride=LEV), :]
        inv = 1.0 / (1.0 + here + kv_t - kv_t * cu_t)
        low = kv_t * inv
        cu_t = here * inv
        at = pl.multiple_of(k * XD, XD)
        cu[pl.ds(at, XD), :] = cu_t
        values = []
        for f in range(FIELDS):
            rows = pl.ds(f * ROWS + at, XD)
            value = sol[rows, :] * inv + low * prev[f]
            sol[rows, :] = value
            values.append(value)
        here_g = gkv[pl.ds(k, 8, stride=LEV), :]
        inv_g = 1.0 / (1.0 + here_g + kv_g - kv_g * cu_g)
        low_g = kv_g * inv_g
        cu_g = here_g * inv_g
        gcu[pl.ds(pl.multiple_of(k * 8, 8), 8), :] = cu_g
        value_g = group[pl.ds(k, 8, stride=LEV), :] * inv_g + low_g * prev_g
        group[pl.ds(k, 8, stride=LEV), :] = value_g
        return here, cu_t, here_g, cu_g, tuple(values), value_g

    zt, zg = jnp.zeros((XD, YD), F32), jnp.zeros((8, 128), F32)
    lax.fori_loop(0, LEV, forward, (zt, zt, zg, zg, (zt,) * FIELDS, zg), unroll=4)

    def backward(i, carry):
        after, after_g = carry
        k = LEV - 1 - i
        at = pl.multiple_of(k * XD, XD)
        cu_t = cu[pl.ds(at, XD), :]
        values = []
        for f in range(FIELDS):
            rows = pl.ds(f * ROWS + at, XD)
            value = sol[rows, :] + cu_t * after[f]
            sol[rows, :] = value
            values.append(value)
        cu_g = gcu[pl.ds(pl.multiple_of(k * 8, 8), 8), :]
        value_g = group[pl.ds(k, 8, stride=LEV), :] + cu_g * after_g
        group[pl.ds(k, 8, stride=LEV), :] = value_g
        return tuple(values), value_g

    lax.fori_loop(0, LEV, backward, ((zt,) * FIELDS, zg), unroll=4)


def couple(phys, mask, group):
    for j in range(8):
        lanes = slice(j * 128, (j + 1) * 128)
        warm, ice = rates(phys[0, :, lanes], phys[1, :, lanes], mask[:, lanes])
        inv = 1.0 / (1.0 + warm + ice)
        passes = group[j * LEV : (j + 1) * LEV, :] * (inv + inv * inv)
        warm, ice = warm * passes, ice * passes
        for f in range(PF):
            phys[f, :, lanes] += COUPLE_WARM[f] * warm + COUPLE_ICE[f] * ice


def update_kernel(recv_b, hot, pre, vap, rest, phys, new_h, phys_h, fin, new, sems):
    top = TOP * ROWS
    copies = [
        pltpu.make_async_copy(rest, new_h.at[pl.ds(top, ALL_ROWS - top)], sems.at[0]),
        pltpu.make_async_copy(phys, phys_h, sems.at[2]),
    ]
    for c in copies:
        c.start()
    warms = t_dot(recv_b[:, 0].reshape(SLOTS, LEV), hot[...])
    ices = t_dot(recv_b[:, 1].reshape(SLOTS, LEV), hot[...])
    for x in range(XD):
        warm, ice = warms[:, x * YD : (x + 1) * YD], ices[:, x * YD : (x + 1) * YD]
        inv = 1.0 / (1.0 + warm + ice)
        rows = [pl.ds(f * ROWS + x, LEV, stride=XD) for f in range(TOP)]
        passes = vap[x] * (inv + inv * inv)
        to_warm, to_ice = warm * passes, ice * passes
        fin[rows[0], :] = pre[rows[0], :] + LATENT_WARM * to_warm + LATENT_ICE * to_ice
        fin[rows[1], :] = pre[rows[1], :] - (to_warm + to_ice)
        fin[rows[2], :] = pre[rows[2], :] + to_warm
        fin[rows[3], :] = pre[rows[3], :] + to_ice
    new[...] = fin[...].astype(BF16)
    copy = pltpu.make_async_copy(new, new_h.at[pl.ds(0, top)], sems.at[1])
    copy.start()
    copies.append(copy)
    for c in copies:
        c.wait()


def shards(atmos_state, horiz_wind, route_map, diffusivity, branch_mask, phys_state):
    q = atmos_state.reshape(ALL_ROWS, YD)
    wind = horiz_wind.reshape(2, ROWS, YD)
    const = jnp.asarray(constants())
    hbm = pl.BlockSpec(memory_space=pltpu.HBM)
    whole = pl.BlockSpec(memory_space=pltpu.VMEM)
    top = TOP * ROWS
    state = pl.pallas_call(
        exchange_kernel,
        out_shape=(
            pltpu.VMEM((COLS, 2, CAP, LEV), BF16),
            pltpu.VMEM((SLOTS, ROWS), BF16),
            pltpu.VMEM((top, YD), F32),
            pltpu.VMEM((XD, LEV, YD), F32),
            pltpu.VMEM((ALL_ROWS - top, YD), BF16),
            pltpu.VMEM((PF, LEV, SLOTS), F32),
        ),
        in_specs=[hbm] * 7,
        out_specs=(whole,) * 6,
        scratch_shapes=[
            pltpu.VMEM((ALL_ROWS, YD), BF16),
            pltpu.VMEM((XD, YD), jnp.int32),
            pltpu.VMEM((LEV, SLOTS), F32),
            pltpu.VMEM((LEV, SLOTS), jnp.int32),
            pltpu.VMEM((2, ROWS, YD), F32),
            pltpu.VMEM((384, 256), BF16),
            pltpu.VMEM((SLOTS, LEV), F32),
            pltpu.SemaphoreType.DMA((7,)),
            pltpu.VMEM((COLS, 2, CAP, LEV), BF16),
            pltpu.VMEM((COLS, 2, CAP, LEV), BF16),
            pltpu.VMEM((COLS, 2, CAP, LEV), BF16),
            pltpu.VMEM((ALL_ROWS, YD), F32),
            pltpu.VMEM((FIELDS, XD, LEV, YD), BF16),
            pltpu.VMEM((ALL_ROWS, YD), F32),
            pltpu.VMEM((2, FIELDS, LEV, YD), BF16),
            pltpu.VMEM((2 * YPAD, ROWS), BF16),
            pltpu.VMEM((2 * YPAD, ROWS), BF16),
            pltpu.VMEM((2, XD, LEV, YD), F32),
            pltpu.VMEM((XD * LEV, YD), F32),
            pltpu.VMEM((ROWS, YD), F32),
            pltpu.VMEM((8 * LEV, 128), F32),
            pltpu.VMEM((8 * LEV, 128), F32),
            pltpu.SemaphoreType.DMA((2, COLS)),
            pltpu.SemaphoreType.DMA((2, COLS)),
            pltpu.SemaphoreType.DMA((4,)),
            pltpu.SemaphoreType.DMA((4,)),
        ],
        compiler_params=pltpu.CompilerParams(
            collective_id=0, has_side_effects=True, vmem_limit_bytes=54 << 20
        ),
    )(q, route_map, diffusivity, branch_mask, phys_state, wind, const)
    new, phys_next = pl.pallas_call(
        update_kernel,
        out_shape=(
            jax.ShapeDtypeStruct((ALL_ROWS, YD), BF16),
            jax.ShapeDtypeStruct((PF, LEV, SLOTS), F32),
        ),
        in_specs=[whole] * 6,
        out_specs=(hbm,) * 2,
        scratch_shapes=[
            pltpu.VMEM((top, YD), F32),
            pltpu.VMEM((top, YD), BF16),
            pltpu.SemaphoreType.DMA((3,)),
        ],
        compiler_params=pltpu.CompilerParams(vmem_limit_bytes=32 << 20),
    )(*state)
    return new.reshape(FIELDS, LEV, XD, YD), phys_next


def solution(mesh):
    return jax.shard_map(
        shards,
        mesh=mesh,
        in_specs=(
            P(None, None, "edge", "cols"),
            P(None, None, "edge", "cols"),
            P("edge", "cols"),
            P(None, ("edge", "cols")),
            P(None, ("edge", "cols")),
            P(None, None, ("edge", "cols")),
        ),
        out_specs=(P(None, None, "edge", "cols"), P(None, None, ("edge", "cols"))),
        check_vma=False,
    )
```

time: 58 us -> 29.1 us (0.50)
  the two profiles are of different devices: /device:TPU:1 before, /device:TPU:29 now
where the time goes in v1:
time: 29.1 us; the launch traced here: 29 us
  Pallas kernels  28.3 us (97%)
  between operations  0.64 us (2%)
    pallas_call x1, Pallas kernels, shards(): pl.pallas_call(exchange_kernel, out_shape=(pltpu.VMEM((COLS, 2, CAP, LEV)...  25.8 us
    pallas_call x1, Pallas kernels, shards(): pl.pallas_call(update_kernel, out_shape=(jax.ShapeDtypeStruct((ALL_ROWS,...  2.5 us

profile of v1, /device:TPU:29, one launch (start us, length us, event | category | flops | bytes accessed | tf_op | source)
XLA Modules:
  0.0 29.0 jit_solution(7745089539981825071)
XLA Ops:
  0.6 25.8 %shard_map.86 = (bf16[32,2,32,128]{3,2,1,0:T(8,128)(2,1)S(1)}, bf16[1024,512]{1,0:T(8,128)(2,1)S(1)}, f32[2048,128]{1,0:T(8,128)S(1)}, f32[4,128,128]{2,1,0:T(8,...) custom-call(bf16[5632,128]{1,0:T(8,128)(2,1)} %bitcast.3, s32[4,128]{1,0:T(4,128)} %route_h.1, ...), custom_call_target="tpu_custom_call" | custom-call | tf_op jit(solution)/shard_map/pallas_call | solution.py:372
  26.4 2.5 %shard_map.87 = (bf16[5632,128]{1,0:T(8,128)(2,1)}, f32[8,128,1024]{2,1,0:T(8,128)}) custom-call(bf16[32,2,32,128]{3,2,1,0:T(8,128)(2,1)S(1)} %get-tuple-element.10.recv_b, bf16[1024,512]{1,0:T(8,128)(2,1)S(1)} %get-tuple-element.11.hot, f32[2048,128]{1,0:T(8,128)S(1)} %get-tuple-element.12.pre, f32[4,128,128]{2,1,0:T(8,128)S(1)} %get-tuple-element.13.vap, ...), custom_call_target="tpu_custom_call" | custom-call | tf_op jit(solution)/shard_map/pallas_call | solution.py:416

commit v2 on v1

--- a/solution.py
+++ b/solution.py
@@ -102,7 +102,7 @@
 def exchange_kernel(
     q_h, route_h, kv_h, mask_h, phys_h, wind_h, const_h,
     recv_b, hot, pre, vap, rest, phys,
-    qv, route, kv, mask, wind, const, group, in_sem,
+    qv, route, kv, mask, wind, const, group, gain, in_sem,
     snd_a, snd_b, recv_a, sol, qp, tn, xr, ys, yr, wp, par, cu, gkv, gcu,
     ss, rs, hss, hrs,
 ):
@@ -120,11 +120,12 @@
         for i, (a, b) in enumerate(
             (
                 (const_h, const), (kv_h, kv), (route_h, route), (q_h, qv),
-                (mask_h, mask), (phys_h, phys), (wind_h, wind),
+                (mask_h, mask), (phys_h.at[pl.ds(0, 2)], phys.at[pl.ds(0, 2)]), (wind_h, wind),
+                (phys_h.at[pl.ds(2, PF - 2)], phys.at[pl.ds(2, PF - 2)]),
             )
         )
     ]
-    for c in loads:
+    for c in loads[:4]:
         c.start()
     bar = pltpu.get_barrier_semaphore()
     for k in order:
@@ -140,8 +141,12 @@
 
     loads[0].wait()
     loads[1].wait()
+    for c in loads[4:7]:
+        c.start()
     for j in range(8):
-        snd_a[4 * j : 4 * j + 4, 0] = turn(j, kv[:, j * 128 : (j + 1) * 128])
+        coupling = kv[:, j * 128 : (j + 1) * 128]
+        snd_a[4 * j : 4 * j + 4, 0] = turn(j, coupling)
+        gkv[pl.ds(j, LEV, stride=8), :] = coupling
 
     loads[2].wait()
     dest_at = lax.broadcasted_iota(jnp.int32, (COLS, YD), 0)
@@ -214,10 +219,13 @@
     for j in range(8):
         lanes = slice(j * 128, (j + 1) * 128)
         warm, ice = rates(phys[0, :, lanes], phys[1, :, lanes], mask[:, lanes])
+        inv = 1.0 / (1.0 + warm + ice)
+        share = inv + inv * inv
+        gain[0, :, lanes] = warm * share
+        gain[1, :, lanes] = ice * share
         snd_b[4 * j : 4 * j + 4, 0] = turn(j, warm)
         snd_b[4 * j : 4 * j + 4, 1] = turn(j, ice)
-    for k in order:
-        message(k, 1).start()
+    loads[7].start()
     recv_a[pl.ds(me, 1)] = snd_a[pl.ds(me, 1)]
     recv_b[pl.ds(me, 1)] = snd_b[pl.ds(me, 1)]
 
@@ -245,6 +253,8 @@
         return carry
 
     lax.fori_loop(0, FIELDS, dynamics, 0)
+    for k in order:
+        message(k, 1).start()
 
     for k in order:
         message(k, 0).wait()
@@ -252,9 +262,8 @@
     for x in range(XD):
         par[x * LEV : (x + 1) * LEV, :] = here[:, x * YD : (x + 1) * YD]
     for j in range(8):
-        rows = pl.ds(j * LEV, LEV)
-        group[rows, :] = dot_t(eye[...], recv_a[4 * j : 4 * j + 4, 1].reshape(128, LEV))
-        gkv[rows, :] = kv[:, j * 128 : (j + 1) * 128]
+        vapour = recv_a[4 * j : 4 * j + 4, 1].reshape(128, LEV)
+        group[pl.ds(j, LEV, stride=8), :] = dot_t(eye[...], vapour)
     solve(sol, par, cu, group, gkv, gcu)
 
     for c in x_copies:
@@ -272,7 +281,8 @@
     for x in range(XD):
         vap[x] = sol[pl.ds(ROWS + x, LEV, stride=XD), :]
     rest[...] = (sol[top:, :] + tn[top:, :]).astype(BF16)
-    couple(phys, mask, group)
+    loads[7].wait()
+    couple(phys, gain, group)
     for k in order:
         message(k, 1).wait()
 
@@ -292,17 +302,18 @@
             value = sol[rows, :] * inv + low * prev[f]
             sol[rows, :] = value
             values.append(value)
-        here_g = gkv[pl.ds(k, 8, stride=LEV), :]
+        at8 = pl.ds(pl.multiple_of(k * 8, 8), 8)
+        here_g = gkv[at8, :]
         inv_g = 1.0 / (1.0 + here_g + kv_g - kv_g * cu_g)
         low_g = kv_g * inv_g
         cu_g = here_g * inv_g
-        gcu[pl.ds(pl.multiple_of(k * 8, 8), 8), :] = cu_g
-        value_g = group[pl.ds(k, 8, stride=LEV), :] * inv_g + low_g * prev_g
-        group[pl.ds(k, 8, stride=LEV), :] = value_g
+        gcu[at8, :] = cu_g
+        value_g = group[at8, :] * inv_g + low_g * prev_g
+        group[at8, :] = value_g
         return here, cu_t, here_g, cu_g, tuple(values), value_g
 
     zt, zg = jnp.zeros((XD, YD), F32), jnp.zeros((8, 128), F32)
-    lax.fori_loop(0, LEV, forward, (zt, zt, zg, zg, (zt,) * FIELDS, zg), unroll=4)
+    lax.fori_loop(0, LEV, forward, (zt, zt, zg, zg, (zt,) * FIELDS, zg), unroll=16)
 
     def backward(i, carry):
         after, after_g = carry
@@ -315,21 +326,19 @@
             value = sol[rows, :] + cu_t * after[f]
             sol[rows, :] = value
             values.append(value)
-        cu_g = gcu[pl.ds(pl.multiple_of(k * 8, 8), 8), :]
-        value_g = group[pl.ds(k, 8, stride=LEV), :] + cu_g * after_g
-        group[pl.ds(k, 8, stride=LEV), :] = value_g
+        at8 = pl.ds(pl.multiple_of(k * 8, 8), 8)
+        value_g = group[at8, :] + gcu[at8, :] * after_g
+        group[at8, :] = value_g
         return tuple(values), value_g
 
-    lax.fori_loop(0, LEV, backward, ((zt,) * FIELDS, zg), unroll=4)
-
-
-def couple(phys, mask, group):
+    lax.fori_loop(0, LEV, backward, ((zt,) * FIELDS, zg), unroll=16)
+
+
+def couple(phys, gain, group):
     for j in range(8):
         lanes = slice(j * 128, (j + 1) * 128)
-        warm, ice = rates(phys[0, :, lanes], phys[1, :, lanes], mask[:, lanes])
-        inv = 1.0 / (1.0 + warm + ice)
-        passes = group[j * LEV : (j + 1) * LEV, :] * (inv + inv * inv)
-        warm, ice = warm * passes, ice * passes
+        vapour = group[pl.ds(j, LEV, stride=8), :]
+        warm, ice = gain[0, :, lanes] * vapour, gain[1, :, lanes] * vapour
         for f in range(PF):
             phys[f, :, lanes] += COUPLE_WARM[f] * warm + COUPLE_ICE[f] * ice
 
@@ -389,7 +398,8 @@
             pltpu.VMEM((2, ROWS, YD), F32),
             pltpu.VMEM((384, 256), BF16),
             pltpu.VMEM((SLOTS, LEV), F32),
-            pltpu.SemaphoreType.DMA((7,)),
+            pltpu.VMEM((2, LEV, SLOTS), F32),
+            pltpu.SemaphoreType.DMA((8,)),
             pltpu.VMEM((COLS, 2, CAP, LEV), BF16),
             pltpu.VMEM((COLS, 2, CAP, LEV), BF16),
             pltpu.VMEM((COLS, 2, CAP, LEV), BF16),

time: 29.1 us -> 26.4 us (0.907)
  the two profiles are of different devices: /device:TPU:29 before, /device:TPU:1 now
where the time goes in v2:
time: 26.4 us; the launch traced here: 26.3 us
  Pallas kernels  25.6 us (97%)
  between operations  0.64 us (2%)
    pallas_call x1, Pallas kernels, shards(): pl.pallas_call(exchange_kernel, out_shape=(pltpu.VMEM((COLS, 2, CAP, LEV)...  23.1 us
    pallas_call x1, Pallas kernels, shards(): pl.pallas_call(update_kernel, out_shape=(jax.ShapeDtypeStruct((ALL_ROWS,...  2.5 us

profile of v2, /device:TPU:1, one launch (start us, length us, event | category | flops | bytes accessed | tf_op | source)
XLA Modules:
  0.0 26.3 jit_solution(13876450854722700416)
XLA Ops:
  0.6 23.1 %shard_map.86 = (bf16[32,2,32,128]{3,2,1,0:T(8,128)(2,1)S(1)}, bf16[1024,512]{1,0:T(8,128)(2,1)S(1)}, f32[2048,128]{1,0:T(8,128)S(1)}, f32[4,128,128]{2,1,0:T(8,...) custom-call(bf16[5632,128]{1,0:T(8,128)(2,1)} %bitcast.3, s32[4,128]{1,0:T(4,128)} %route_h.1, ...), custom_call_target="tpu_custom_call" | custom-call | tf_op jit(solution)/shard_map/pallas_call | solution.py:381
  23.8 2.5 %shard_map.87 = (bf16[5632,128]{1,0:T(8,128)(2,1)}, f32[8,128,1024]{2,1,0:T(8,128)}) custom-call(bf16[32,2,32,128]{3,2,1,0:T(8,128)(2,1)S(1)} %get-tuple-element.10.recv_b, bf16[1024,512]{1,0:T(8,128)(2,1)S(1)} %get-tuple-element.11.hot, f32[2048,128]{1,0:T(8,128)S(1)} %get-tuple-element.12.pre, f32[4,128,128]{2,1,0:T(8,128)S(1)} %get-tuple-element.13.vap, ...), custom_call_target="tpu_custom_call" | custom-call | tf_op jit(solution)/shard_map/pallas_call | solution.py:426

commit v3 on v2

--- a/solution.py
+++ b/solution.py
@@ -208,9 +208,17 @@
         to = peer(k)
         source, target = ((snd_a, recv_a), (snd_b, recv_b))[part]
         return pltpu.make_async_remote_copy(
-            source.at[to], target.at[me], ss.at[part, k], rs.at[part, k],
+            source.at[to], target.at[me], ss.at[part], rs.at[part],
             device_id=(e, to), device_id_type=MESH,
         )
+
+    def settle(part):
+        source, target = ((snd_a, recv_a), (snd_b, recv_b))[part]
+        others = pl.ds(0, COLS - 1)
+        pltpu.make_async_remote_copy(
+            source.at[others], target.at[others], ss.at[part], rs.at[part],
+            device_id=(e, peer(1)), device_id_type=MESH,
+        ).wait()
 
     for k in order:
         message(k, 0).start()
@@ -256,8 +264,7 @@
     for k in order:
         message(k, 1).start()
 
-    for k in order:
-        message(k, 0).wait()
+    settle(0)
     here = t_dot(recv_a[:, 0].reshape(SLOTS, LEV), hot[...])
     for x in range(XD):
         par[x * LEV : (x + 1) * LEV, :] = here[:, x * YD : (x + 1) * YD]
@@ -266,6 +273,8 @@
         group[pl.ds(j, LEV, stride=8), :] = dot_t(eye[...], vapour)
     solve(sol, par, cu, group, gkv, gcu)
 
+    loads[7].wait()
+    couple(phys, gain, group)
     for c in x_copies:
         c.wait()
 
@@ -281,10 +290,7 @@
     for x in range(XD):
         vap[x] = sol[pl.ds(ROWS + x, LEV, stride=XD), :]
     rest[...] = (sol[top:, :] + tn[top:, :]).astype(BF16)
-    loads[7].wait()
-    couple(phys, gain, group)
-    for k in order:
-        message(k, 1).wait()
+    settle(1)
 
 
 def solve(sol, par, cu, group, gkv, gcu):
@@ -351,22 +357,23 @@
     ]
     for c in copies:
         c.start()
-    warms = t_dot(recv_b[:, 0].reshape(SLOTS, LEV), hot[...])
-    ices = t_dot(recv_b[:, 1].reshape(SLOTS, LEV), hot[...])
+    both = jnp.concatenate([recv_b[:, i].reshape(SLOTS, LEV) for i in range(2)], axis=1)
+    both = t_dot(both, hot[...])
     for x in range(XD):
-        warm, ice = warms[:, x * YD : (x + 1) * YD], ices[:, x * YD : (x + 1) * YD]
+        warm, ice = both[:LEV, x * YD : (x + 1) * YD], both[LEV:, x * YD : (x + 1) * YD]
         inv = 1.0 / (1.0 + warm + ice)
-        rows = [pl.ds(f * ROWS + x, LEV, stride=XD) for f in range(TOP)]
         passes = vap[x] * (inv + inv * inv)
-        to_warm, to_ice = warm * passes, ice * passes
-        fin[rows[0], :] = pre[rows[0], :] + LATENT_WARM * to_warm + LATENT_ICE * to_ice
-        fin[rows[1], :] = pre[rows[1], :] - (to_warm + to_ice)
-        fin[rows[2], :] = pre[rows[2], :] + to_warm
-        fin[rows[3], :] = pre[rows[3], :] + to_ice
-    new[...] = fin[...].astype(BF16)
-    copy = pltpu.make_async_copy(new, new_h.at[pl.ds(0, top)], sems.at[1])
-    copy.start()
-    copies.append(copy)
+        warm, ice = warm * passes, ice * passes
+        gains = (LATENT_WARM * warm + LATENT_ICE * ice, -(warm + ice), warm, ice)
+        for f in range(TOP):
+            rows = pl.ds(f * ROWS + x, LEV, stride=XD)
+            fin[rows, :] = pre[rows, :] + gains[f]
+    for f in range(TOP):
+        rows = pl.ds(f * ROWS, ROWS)
+        new[rows, :] = fin[rows, :].astype(BF16)
+        copy = pltpu.make_async_copy(new.at[rows], new_h.at[rows], sems.at[3 + f])
+        copy.start()
+        copies.append(copy)
     for c in copies:
         c.wait()
 
@@ -414,8 +421,8 @@
             pltpu.VMEM((ROWS, YD), F32),
             pltpu.VMEM((8 * LEV, 128), F32),
             pltpu.VMEM((8 * LEV, 128), F32),
-            pltpu.SemaphoreType.DMA((2, COLS)),
-            pltpu.SemaphoreType.DMA((2, COLS)),
+            pltpu.SemaphoreType.DMA((2,)),
+            pltpu.SemaphoreType.DMA((2,)),
             pltpu.SemaphoreType.DMA((4,)),
             pltpu.SemaphoreType.DMA((4,)),
         ],
@@ -434,7 +441,7 @@
         scratch_shapes=[
             pltpu.VMEM((top, YD), F32),
             pltpu.VMEM((top, YD), BF16),
-            pltpu.SemaphoreType.DMA((3,)),
+            pltpu.SemaphoreType.DMA((3 + TOP,)),
         ],
         compiler_params=pltpu.CompilerParams(vmem_limit_bytes=32 << 20),
     )(*state)

time: 26.4 us -> 25.3 us (0.958)
  Pallas kernels: 25.6 us -> 24.5 us
    pallas_call x1, Pallas kernels: 23.1 us -> 22 us  [shards(): pl.pallas_call(exchange_kernel, out_shape=(pltpu.VMEM((COLS, 2, CAP, LEV)...]
where the time goes in v3:
time: 25.3 us; the launch traced here: 25.1 us
  Pallas kernels  24.5 us (97%)
  between operations  0.64 us (3%)
    pallas_call x1, Pallas kernels, shards(): pl.pallas_call(exchange_kernel, out_shape=(pltpu.VMEM((COLS, 2, CAP, LEV)...  22 us
    pallas_call x1, Pallas kernels, shards(): pl.pallas_call(update_kernel, out_shape=(jax.ShapeDtypeStruct((ALL_ROWS,...  2.52 us

profile of v3, /device:TPU:1, one launch (start us, length us, event | category | flops | bytes accessed | tf_op | source)
XLA Modules:
  0.0 25.1 jit_solution(1704946671069402385)
XLA Ops:
  0.6 22.0 %shard_map.86 = (bf16[32,2,32,128]{3,2,1,0:T(8,128)(2,1)S(1)}, bf16[1024,512]{1,0:T(8,128)(2,1)S(1)}, f32[2048,128]{1,0:T(8,128)S(1)}, f32[4,128,128]{2,1,0:T(8,...) custom-call(bf16[5632,128]{1,0:T(8,128)(2,1)} %bitcast.3, s32[4,128]{1,0:T(4,128)} %route_h.1, ...), custom_call_target="tpu_custom_call" | custom-call | tf_op jit(solution)/shard_map/pallas_call | solution.py:388
  22.6 2.5 %shard_map.87 = (bf16[5632,128]{1,0:T(8,128)(2,1)}, f32[8,128,1024]{2,1,0:T(8,128)}) custom-call(bf16[32,2,32,128]{3,2,1,0:T(8,128)(2,1)S(1)} %get-tuple-element.10.recv_b, bf16[1024,512]{1,0:T(8,128)(2,1)S(1)} %get-tuple-element.11.hot, f32[2048,128]{1,0:T(8,128)S(1)} %get-tuple-element.12.pre, f32[4,128,128]{2,1,0:T(8,128)S(1)} %get-tuple-element.13.vap, ...), custom_call_target="tpu_custom_call" | custom-call | tf_op jit(solution)/shard_map/pallas_call | solution.py:433

commit v4 on v3

--- a/solution.py
+++ b/solution.py
@@ -128,7 +128,7 @@
     for c in loads[:4]:
         c.start()
     bar = pltpu.get_barrier_semaphore()
-    for k in order:
+    for k in order[::-1]:
         pl.semaphore_signal(bar, inc=1, device_id=(e, peer(k)), device_id_type=MESH)
     for to in (up_x, down_x):
         pl.semaphore_signal(bar, inc=1, device_id=(to, me), device_id_type=MESH)

time: 25.3 us -> 25.3 us (level)
  no operation moved by 1% of the time
where the time goes in v4:
time: 25.3 us; the launch traced here: 25.2 us
  Pallas kernels  24.5 us (97%)
  between operations  0.64 us (3%)
    pallas_call x1, Pallas kernels, shards(): pl.pallas_call(exchange_kernel, out_shape=(pltpu.VMEM((COLS, 2, CAP, LEV)...  22 us
    pallas_call x1, Pallas kernels, shards(): pl.pallas_call(update_kernel, out_shape=(jax.ShapeDtypeStruct((ALL_ROWS,...  2.52 us

profile of v4, /device:TPU:1, one launch (start us, length us, event | category | flops | bytes accessed | tf_op | source)
XLA Modules:
  0.0 25.2 jit_solution(6200417831564066576)
XLA Ops:
  0.6 22.0 %shard_map.86 = (bf16[32,2,32,128]{3,2,1,0:T(8,128)(2,1)S(1)}, bf16[1024,512]{1,0:T(8,128)(2,1)S(1)}, f32[2048,128]{1,0:T(8,128)S(1)}, f32[4,128,128]{2,1,0:T(8,...) custom-call(bf16[5632,128]{1,0:T(8,128)(2,1)} %bitcast.3, s32[4,128]{1,0:T(4,128)} %route_h.1, ...), custom_call_target="tpu_custom_call" | custom-call | tf_op jit(solution)/shard_map/pallas_call | solution.py:388
  22.6 2.5 %shard_map.87 = (bf16[5632,128]{1,0:T(8,128)(2,1)}, f32[8,128,1024]{2,1,0:T(8,128)}) custom-call(bf16[32,2,32,128]{3,2,1,0:T(8,128)(2,1)S(1)} %get-tuple-element.10.recv_b, bf16[1024,512]{1,0:T(8,128)(2,1)S(1)} %get-tuple-element.11.hot, f32[2048,128]{1,0:T(8,128)S(1)} %get-tuple-element.12.pre, f32[4,128,128]{2,1,0:T(8,128)S(1)} %get-tuple-element.13.vap, ...), custom_call_target="tpu_custom_call" | custom-call | tf_op jit(solution)/shard_map/pallas_call | solution.py:433
